TPU v7x, 32 devices: a whole 2x2x4 slice. The times are simulated.
32 devices in a mesh: mp: 2 (over core), heads: 8 (over z, y), tok: 2 (over x).
Axes of the slice: x: 2, y: 2, z: 4, core: 2. Of those that a mesh axis runs over, the one named last changes fastest.
Arguments:
- context: bfloat16 [2, 512, 8192], P('mp', None, 'heads'), may hold values from -6 to 6
- out_weight: bfloat16 [2, 8192, 8192], P('mp', 'heads', 'tok'), may hold values from -0.0625 to 0.0625
- skip_states: bfloat16 [2, 512, 8192], P(None, None, 'tok'), may hold values from -6 to 6
- gram_old: float32 [8192, 8192], P('tok', ('mp', 'heads')), may hold values from -1 to 3
- cross_old: float32 [8192, 8192], P('tok', ('mp', 'heads')), may hold values from -30 to 30
- map_old: float32 [8192, 8192], P('tok', ('mp', 'heads')), may hold values from -0.3 to 0.3
Outputs:
- gram_new: float32 [8192, 8192], P('tok', ('mp', 'heads'))
- cross_new: float32 [8192, 8192], P('tok', ('mp', 'heads'))
- map_new: float32 [8192, 8192], P('tok', ('mp', 'heads'))
- residual_new: float32 [8192, 8192], P('tok', ('mp', 'heads'))
All inputs are finite; a program needn't handle non-finite values.
Results may differ from a plain program's by a relative error of at most 0.03.
Values may be sent and summed in bfloat16 or wider, within the bound.
A program may use at most 256 MiB of HBM per device.

v0:
```python
import jax
import jax.numpy as jnp
from jax import lax
from jax.sharding import PartitionSpec as P

decay_keep = 0.75
ridge_weight = 0.1


def from_root(block, axis, holder):
    block = jnp.where(lax.axis_index(axis) == holder, block, jnp.zeros_like(block))
    return lax.psum(block, axis)


def columns(matrix):
    return lax.all_gather(matrix, "tok", axis=0, tiled=True)


def token_inner(left, right):
    return lax.dot_general(
        left, right, (((0,), (0,)), ((), ())), preferred_element_type=jnp.float32
    )


def per_device(context, out_weight, skip_states, gram_old, cross_old, map_old):
    tokens = context.shape[1]
    width_a = gram_old.shape[0]
    width_c = gram_old.shape[1]
    partial_value = jnp.dot(context[0], out_weight[0], preferred_element_type=jnp.float32)
    model_index = lax.axis_index("mp")
    slot_mask = jnp.arange(2, dtype=jnp.int32) == model_index
    slot_terms = jnp.where(slot_mask[:, None, None], partial_value[None, :, :], 0.0)
    summed = lax.psum(slot_terms.astype(jnp.bfloat16), ("mp", "heads")).astype(jnp.float32)
    states = (summed + skip_states.astype(jnp.float32)).astype(jnp.bfloat16)
    source = states[0]
    target = states[1]
    column = lax.axis_index(("mp", "heads"))
    root_index = column * width_c // width_a
    offset = column * width_c - root_index * width_a
    picked = jnp.stack(
        [
            lax.dynamic_slice_in_dim(source, offset, width_c, 1),
            lax.dynamic_slice_in_dim(target, offset, width_c, 1),
        ]
    )
    fetched = from_root(picked, "tok", root_index)
    new_weight = (1.0 - decay_keep) / tokens
    gram_new = decay_keep * gram_old + new_weight * token_inner(source, fetched[0])
    cross_new = decay_keep * cross_old + new_weight * token_inner(source, fetched[1])
    gram_half = gram_new.astype(jnp.bfloat16)
    map_half = map_old.astype(jnp.bfloat16)
    row_panel = lax.all_gather(gram_half, ("mp", "heads"), axis=1, tiled=True)

    def apply_gram(matrix):
        return jnp.dot(row_panel, columns(matrix), preferred_element_type=jnp.float32)

    residual = cross_new - apply_gram(map_half) - ridge_weight * map_old
    applied = apply_gram(residual.astype(jnp.bfloat16)) + ridge_weight * residual
    totals = lax.psum(
        (jnp.sum(residual * residual), jnp.sum(residual * applied)), ("mp", "heads", "tok")
    )
    step_size = totals[0] / totals[1]
    return (gram_new, cross_new, map_old + step_size * residual, residual - step_size * applied)


def solution(mesh):
    placed = (
        P("mp", None, "heads"),
        P("mp", "heads", "tok"),
        P(None, None, "tok"),
        P("tok", ("mp", "heads")),
        P("tok", ("mp", "heads")),
        P("tok", ("mp", "heads")),
    )
    return jax.shard_map(
        per_device,
        mesh=mesh,
        in_specs=placed,
        out_specs=(
            P("tok", ("mp", "heads")),
            P("tok", ("mp", "heads")),
            P("tok", ("mp", "heads")),
            P("tok", ("mp", "heads")),
        ),
        check_vma=False,
    )
```

profile of v0, /device:TPU:0, one launch (start us, length us, event | category | flops | bytes accessed | tf_op | source)
XLA Modules:
  0.0 940.5 jit_solution(4489660221661309988)
XLA Ops:
  7.2 1.2 copy-done
  8.4 8.1 fusion
  16.5 5.4 select_convert_fusion
  21.9 0.0 all-reduce.6.cloned.1.call-start
  22.0 172.7 %all-reduce.4.cloned.1.call-done = bf16[2,512,4096]{2,1,0:T(8,128)(2,1)} async-done(((bf16[2,512,4096]{2,1,0:T(8,128)(2,1)}), bf16[2,512,4096]{2,1,0:T(8,128)(2,1)}) %all-reduce.4.cloned.1.call-update) | async-done | bytes 8388624 | tf_op jit(solution)/shard_map/psum | solution.py:33
  194.7 7.5 add_convert_fusion
  202.2 1.0 fusion.7
  203.3 2.4 copy-done.2
  205.6 0.1 constant_dynamic-slice_fusion
  205.7 1.1 maximum_select_fusion
  206.8 0.0 all-gather.6.cloned.1.call-start
  206.9 5.9 convert_element_type.26
  212.8 0.0 all-gather.4.cloned.1.call-start
  212.9 34.0 %all-reduce.6.cloned.1.call-done = bf16[2,512,512]{2,1,0:T(8,128)(2,1)} async-done(((bf16[2,512,512]{2,1,0:T(8,128)(2,1)}), bf16[2,512,512]{2,1,0:T(8,128)(2,1)}) %all-reduce.6.cloned.1.call-update) | async-done | bytes 1048592 | tf_op jit(solution)/shard_map/psum | solution.py:12
  246.9 13.9 %fusion.8 = (bf16[4096,512]{1,0:T(8,128)(2,1)}, f32[4096,512]{1,0:T(8,128)}) fusion(bf16[2,512,512]{2,1,0:T(8,128)(2,1)} %all-reduce.6.cloned.1.call-done, bf16[2,512,4096]{2,1,0:T(8,128)(2,1)} %copy-done.2, f32[4096,512]{1,0:T(8,128)} %param.9), kind=kOutput, calls=%fused_computation.24 | convolution fusion | flops 2155872256 | bytes 25690112 | tf_op jit(solution)/shard_map/dot_general | solution.py:20
  260.8 0.2 all-gather.8.cloned.1.call-start
  261.0 11.7 %multiply_add_fusion.2 = f32[4096,512]{1,0:T(8,128)} fusion(f32[4096,512]{1,0:T(8,128)} %param.10, bf16[2,512,512]{2,1,0:T(8,128)(2,1)S(1)} %copy-done.3, bf16[2,512,4096]{2,1,0:T(8,128)(2,1)} %copy-done.2), kind=kOutput, calls=%fused_computation.10 | convolution fusion | flops 2153775104 | bytes 21495808 | tf_op jit(solution)/shard_map/dot_general | solution.py:20
  272.7 79.7 %all-gather.6.cloned.1.call-done = bf16[8192,512]{1,0:T(8,128)(2,1)} async-done(((bf16[4096,512]{1,0:T(8,128)(2,1)}), bf16[8192,512]{1,0:T(8,128)(2,1)}) %all-gather.6.cloned.1.call-update) | async-done | bytes 8388624 | tf_op jit(solution)/shard_map/all_gather | solution.py:16
  352.5 328.2 %all-gather.4.cloned.1.call-done = bf16[4096,8192]{1,0:T(8,128)(2,1)} async-done(((bf16[4096,512]{1,0:T(8,128)(2,1)}), bf16[4096,8192]{1,0:T(8,128)(2,1)}) %all-gather.4.cloned.1.call-update) | async-done | bytes 67108880 | tf_op jit(solution)/shard_map/all_gather | solution.py:52
  680.7 47.0 %fusion.9 = (bf16[4096,512]{1,0:T(8,128)(2,1)}, f32[4096,512]{1,0:T(8,128)}) fusion(f32[4096,512]{1,0:T(8,128)} %param.11, f32[4096,512]{1,0:T(8,128)} %multiply_add_fusion.2, bf16[4096,8192]{1,0:T(8,128)(2,1)} %all-gather.4.cloned.1.call-done, bf16[8192,512]{1,0:T(8,128)(2,1)} %all-gather.6.cloned.1.call-done), kind=kOutput, calls=%fused_computation.25 | convolution fusion | flops 34368126976 | bytes 104857600 | tf_op jit(solution)/shard_map/dot_general | solution.py:55
  727.7 104.1 %all-gather.8.cloned.1.call-done = bf16[8192,512]{1,0:T(8,128)(2,1)} async-done(((bf16[4096,512]{1,0:T(8,128)(2,1)}), bf16[8192,512]{1,0:T(8,128)(2,1)}) %all-gather.8.cloned.1.call-update) | async-done | bytes 8388624 | tf_op jit(solution)/shard_map/all_gather | solution.py:16
  831.8 45.8 %multiply_reduce_fusion = (f32[]{:T(128)}, f32[]{:T(128)}, f32[4096,512]{1,0:T(8,128)}) fusion(f32[4096,512]{1,0:T(8,128)} %get-tuple-element.15, bf16[4096,8192]{1,0:T(8,128)(2,1)} %all-gather.4.cloned.1.call-done, bf16[8192,512]{1,0:T(8,128)(2,1)} %all-gather.8.cloned.1.call-done), kind=kOutput, calls=%fused_computation.6 | convolution fusion | flops 34372321280 | bytes 92274696 | tf_op jit(solution)/shard_map/dot_general | solution.py:55
  877.6 39.6 %all-reduce = (f32[]{:T(128)}, f32[]{:T(128)}) all-reduce(f32[]{:T(128)} %get-tuple-element.5, f32[]{:T(128)} %get-tuple-element.4), channel_id=1, replica_groups=mesh['mp'=2,'heads'=8,'tok'=2] {'mp','heads','tok'}, use_global_device_ids=true, to_apply=%region_3.4 | all-reduce | flops 2 | bytes 16 | tf_op jit(solution)/shard_map/psum | solution.py:59
  918.5 15.5 %multiply_subtract_fusion = (f32[4096,512]{1,0:T(8,128)}, f32[4096,512]{1,0:T(8,128)}) fusion(f32[4096,512]{1,0:T(8,128)} %get-tuple-element.15, f32[4096,512]{1,0:T(8,128)} %get-tuple-element.16, f32[]{:T(128)S(6)} %div.14, f32[4096,512]{1,0:T(8,128)} %param.11), kind=kLoop, calls=%fused_computation.4 | loop fusion | flops 12582912 | bytes 41943044 | tf_op jit(solution)/shard_map/sub | solution.py:63
  (13 shorter events, 0.1 us)
Async XLA Ops:
  7.2 1.2 copy-start
  7.2 187.5 %all-reduce.4.cloned.1.call-start = ((), (), s32[]{:S(2)}) async-start(), calls=%async_computation | async-start | bytes 16777216 | tf_op jit(solution)/shard_map/psum | solution.py:33
  21.9 224.9 %all-reduce.6.cloned.1.call-start = ((), (), s32[]{:S(2)}) async-start(), calls=%async_computation.1 | async-start | bytes 2097152 | tf_op jit(solution)/shard_map/psum | solution.py:12
  202.2 3.4 copy-start.2
  206.8 145.6 %all-gather.6.cloned.1.call-start = ((), (), s32[]{:S(2)}) async-start(), calls=%async_computation.3 | async-start | bytes 12582912 | tf_op jit(solution)/shard_map/all_gather | solution.py:16
  212.8 467.8 %all-gather.4.cloned.1.call-start = ((), (), s32[]{:S(2)}) async-start(), calls=%async_computation.2 | async-start | bytes 71303168 | tf_op jit(solution)/shard_map/all_gather | solution.py:52
  246.9 14.1 %copy-start.3 = (bf16[2,512,512]{2,1,0:T(8,128)(2,1)S(1)}, bf16[2,512,512]{2,1,0:T(8,128)(2,1)}, u32[]{:S(2)}) copy-start(bf16[2,512,512]{2,1,0:T(8,128)(2,1)} %all-reduce.6.cloned.1.call-done) | copy-start | bytes 3145732
  260.8 571.1 %all-gather.8.cloned.1.call-start = ((), (), s32[]{:S(2)}) async-start(), calls=%async_computation.4 | async-start | bytes 12582912 | tf_op jit(solution)/shard_map/all_gather | solution.py:16
  918.5 15.5 %copy-start.1 = (bf16[1,512,1024]{2,1,0:T(8,128)(2,1)S(1)}, bf16[1,512,1024]{2,1,0:T(8,128)(2,1)}, u32[]{:S(2)}) copy-start(bf16[1,512,1024]{2,1,0:T(8,128)(2,1)} %param.6) | copy-start | bytes 3145732
Sparse Core Ops, SparseCore 0:
  22.1 172.6 all-reduce.3
  207.0 39.8 all-reduce.5
  248.4 103.9 all-gather.5
  354.5 326.1 all-gather.3
  727.8 103.9 all-gather.7
where the time goes:
time: 941 us
  waiting for transfers between devices  719 us (76%)
  matrix products  126 us (13%)
  blocking collectives  39.6 us (4%)
  other arithmetic  35.4 us (4%)
  between operations  15.2 us (2%)
    all_gather x1, waiting for transfers between devices, per_device(): row_panel = lax.all_gather(gram_half, ('mp', 'heads'), axis=1, tiled=True)  328 us
    all_gather x2, waiting for transfers between devices, columns(): return lax.all_gather(matrix, 'tok', axis=0, tiled=True)  184 us
    psum x1, waiting for transfers between devices, per_device(): lax.psum(slot_terms.astype(jnp.bfloat16), ('mp', 'heads'))  173 us
    dot_general x2, matrix products, apply_gram(): jnp.dot(row_panel, columns(matrix), preferred_element_type=jnp.float32)  92.8 us
    psum x1, blocking collectives, per_device(): lax.psum((jnp.sum(residual * residual), jnp.sum(residual * applied)), ('m...  39.6 us
    psum x1, waiting for transfers between devices, from_root(): return lax.psum(block, axis)  34 us
    dot_general x2, matrix products, token_inner(): lax.dot_general(left, right, (((0,), (0,)), ((), ())), preferred_element_...  25.6 us
  transfers between devices with their start and end apart: 5, of which 5 were waited for; matrix products, arithmetic and copies ran while one was open for 3% of the time, Pallas kernels for 0%

commit v1 on v0

v1 whole, which is shorter than its diff:
```python
import jax
import jax.numpy as jnp
from jax import lax
from jax.sharding import PartitionSpec as P

decay_keep = 0.75
ridge_weight = 0.1
f32, bf16 = jnp.float32, jnp.bfloat16
CHUNKS = 4


def dot(a, b):
    return jnp.dot(a, b, preferred_element_type=f32)


def token_inner(left, right):
    return lax.dot_general(left, right, (((0,), (0,)), ((), ())), preferred_element_type=f32)


def shifted(block, axis, shift):
    n = lax.axis_size(axis)
    return lax.ppermute(block, axis, [(i, (i + shift) % n) for i in range(n)])


def total_over(value, axis):
    n = lax.axis_size(axis)
    if n & (n - 1):
        return lax.psum(value, axis)
    bit = 1
    while bit < n:
        value = value + lax.ppermute(value, axis, [(i, i ^ bit) for i in range(n)])
        bit *= 2
    return value


def sum_tok(value):
    n = lax.axis_size("tok")
    half = value.astype(bf16)
    for shift in range(1, n):
        value = value + shifted(half, "tok", shift).astype(f32)
    return value.astype(bf16)


def make_states(context, out_weight, skip_states, width):
    n_tok, n_heads, n_mp = (lax.axis_size(a) for a in ("tok", "heads", "mp"))
    t, h, k = (lax.axis_index(a) for a in ("tok", "heads", "mp"))
    tokens, features = skip_states.shape[1:]
    share = features // n_heads
    part = dot(context[0], out_weight[0]).astype(bf16)
    mine = lax.psum_scatter(part, "heads", scatter_dimension=1, tiled=True)
    skip = lax.dynamic_slice(skip_states, (k, 0, h * share), (1, tokens, share))[0]
    mine = (mine.astype(f32) + skip.astype(f32)).astype(bf16)
    other = lax.ppermute(mine, "mp", [(0, 1), (1, 0)])
    pair = jnp.stack([jnp.where(k == 0, mine, other), jnp.where(k == 0, other, mine)])
    if share == width and n_tok == n_mp == 2:
        away = lax.ppermute(pair, ("mp", "tok"), [(0, 1), (3, 2)])
        columns = jnp.where(k == t, pair, away)
        half = lax.dynamic_slice_in_dim(pair[0], k * (tokens // 2), tokens // 2, 0)
        rows = lax.all_gather(half, "heads", axis=1, tiled=True)
        rows_other = lax.ppermute(rows, "mp", [(0, 1), (1, 0)])
        first = jnp.where(k == 0, rows, rows_other)
        second = jnp.where(k == 0, rows_other, rows)
        source = jnp.concatenate([first, second], 0)
        return source, columns[0], columns[1]
    both = lax.all_gather(pair, "heads", axis=2, tiled=True)
    whole = lax.all_gather(both, "tok", axis=2, tiled=True)
    columns = lax.dynamic_slice_in_dim(whole, (k * n_heads + h) * width, width, 2)
    return both[0], columns[0], columns[1]


def per_device(context, out_weight, skip_states, gram_old, cross_old, map_old):
    n_tok = lax.axis_size("tok")
    t = lax.axis_index("tok")
    tokens = context.shape[1]
    height, width = gram_old.shape
    new_weight = (1.0 - decay_keep) / tokens
    step = height // CHUNKS
    cuts = [slice(c * step, (c + 1) * step) for c in range(CHUNKS)]

    map_half = map_old.astype(bf16)
    gram_old_half = gram_old.astype(bf16)
    panels = [lax.all_gather(gram_old_half[cut], ("mp", "heads"), axis=1, tiled=True) for cut in cuts]
    maps = [map_half] + [shifted(map_half, "tok", s) for s in range(1, n_tok)]
    source, source_cols, target_cols = make_states(context, out_weight, skip_states, width)

    gram_new = decay_keep * gram_old + new_weight * token_inner(source, source_cols)
    cross_new = decay_keep * cross_old + new_weight * token_inner(source, target_cols)

    def panel_part(panel, s):
        owner = lax.rem(t - s + n_tok, n_tok)
        return lax.dynamic_slice_in_dim(panel, owner * height, height, 1)

    inner_map = sum_tok(dot(source, map_half))
    residuals, halves = [], []
    for cut, panel in zip(cuts, panels):
        product = sum(dot(panel_part(panel, s), maps[s]) for s in range(n_tok))
        low_rank = token_inner(source[:, cut], inner_map)
        residual = (
            cross_new[cut] - decay_keep * product - new_weight * low_rank - ridge_weight * map_old[cut]
        )
        residuals.append(residual)
        halves.append(residual.astype(bf16))
    away = [[shifted(half, "tok", s) for half in halves] for s in range(1, n_tok)]
    inner_residual = sum_tok(sum(dot(source[:, cut], half) for cut, half in zip(cuts, halves)))
    blocks = [jnp.concatenate(halves, 0)] + [jnp.concatenate(a, 0) for a in away]
    applied, squares, mixed = [], 0.0, 0.0
    for cut, panel, residual in zip(cuts, panels, residuals):
        product = sum(dot(panel_part(panel, s), blocks[s]) for s in range(n_tok))
        low_rank = token_inner(source[:, cut], inner_residual)
        value = decay_keep * product + new_weight * low_rank + ridge_weight * residual
        applied.append(value)
        squares = squares + jnp.sum(residual * residual)
        mixed = mixed + jnp.sum(residual * value)
    totals = jnp.stack([squares, mixed])
    for axis in ("mp", "tok", "heads"):
        totals = total_over(totals, axis)
    step_size = totals[0] / totals[1]
    residual = jnp.concatenate(residuals, 0)
    return (
        gram_new,
        cross_new,
        map_old + step_size * residual,
        residual - step_size * jnp.concatenate(applied, 0),
    )


def solution(mesh):
    block = P("tok", ("mp", "heads"))
    placed = (P("mp", None, "heads"), P("mp", "heads", "tok"), P(None, None, "tok"), block, block, block)
    return jax.shard_map(
        per_device, mesh=mesh, in_specs=placed, out_specs=(block,) * 4, check_vma=False
    )
```

time: 941 us -> 848 us (0.901)
  waiting for transfers between devices: 719 us -> 562 us
  matrix products: 126 us -> 196 us
  blocking collectives: 39.6 us -> 0 us
  starting transfers between devices: 0.39 us -> 17.1 us
  local copies, waits for them, and re-layouts: 4.66 us -> 15.3 us
    psum x2 -> x0, waiting for transfers between devices: 207 us -> none  [the longest x1 173 us: per_device(): lax.psum(slot_terms.astype(jnp.bfloat16), ('mp', 'heads'))]
    all_gather x3 -> x5, waiting for transfers between devices: 512 us -> 371 us  [the longest x4 327 us: per_device(): lax.all_gather(gram_old_half[cut], ('mp', 'heads'), axis=1, tiled=True)]
    ppermute x0 -> x15, waiting for transfers between devices: none -> 98.2 us  [the longest x7 73.2 us: shifted(): return lax.ppermute(block, axis, [(i, (i + shift) % n) for i in range(n)])]
    reduce_scatter x0 -> x1, waiting for transfers between devices: none -> 91.3 us  [make_states(): mine = lax.psum_scatter(part, 'heads', scatter_dimension=1, tiled=True)]
    dot_general x3 -> x22, matrix products: 101 us -> 154 us  [dot(): return jnp.dot(a, b, preferred_element_type=f32)]
    psum x1 -> x0, blocking collectives: 39.6 us -> none  [per_device(): lax.psum((jnp.sum(residual * residual), jnp.sum(residual * applied)), ('m...]
    ppermute x0 -> x15, starting transfers between devices: none -> 16.8 us  [the longest x7 8.9 us: shifted(): return lax.ppermute(block, axis, [(i, (i + shift) % n) for i in range(n)])]
    dot_general x2 -> x10, matrix products: 25.6 us -> 41.5 us  [token_inner(): lax.dot_general(left, right, (((0,), (0,)), ((), ())), preferred_element_...]
  transfers between devices with their start and end apart: 5 -> 21, of which waited for: 5 -> 14; matrix products, arithmetic and copies ran while one was open for 3% -> 19% of each run, Pallas kernels for 0% -> 0%
where the time goes in v1:
time: 848 us; the launch traced here: 842 us
  waiting for transfers between devices  562 us (66%)
  matrix products  196 us (23%)
  other arithmetic  30.7 us (4%)
  between operations  21.5 us (3%)
  starting transfers between devices  17.1 us (2%)
  local copies, waits for them, and re-layouts  15.3 us (2%)
    all_gather x4, waiting for transfers between devices, per_device(): lax.all_gather(gram_old_half[cut], ('mp', 'heads'), axis=1, tiled=True)  327 us
    dot_general x22, matrix products, dot(): return jnp.dot(a, b, preferred_element_type=f32)  154 us
    reduce_scatter x1, waiting for transfers between devices, make_states(): mine = lax.psum_scatter(part, 'heads', scatter_dimension=1, tiled=True)  91.3 us
    ppermute x7, waiting for transfers between devices, shifted(): return lax.ppermute(block, axis, [(i, (i + shift) % n) for i in range(n)])  73.2 us
    all_gather x1, waiting for transfers between devices, make_states(): rows = lax.all_gather(half, 'heads', axis=1, tiled=True)  43.2 us
    dot_general x10, matrix products, token_inner(): lax.dot_general(left, right, (((0,), (0,)), ((), ())), preferred_element_...  41.5 us
  transfers between devices with their start and end apart: 21, of which 14 were waited for; matrix products, arithmetic and copies ran while one was open for 19% of the time, Pallas kernels for 0%

profile of v1, /device:TPU:0, one launch (start us, length us, event | category | flops | bytes accessed | tf_op | source)
XLA Modules:
  0.0 842.2 jit_solution(6807376808990272788)
XLA Ops:
  8.4 9.4 %fusion.35 = bf16[512,4096]{1,0:T(8,128)(2,1)} fusion(bf16[1,1024,4096]{2,1,0:T(8,128)(2,1)} %param.7, bf16[1,512,1024]{2,1,0:T(8,128)(2,1)S(1)} %copy-done), kind=kOutput, calls=%fused_computation.49 | convolution fusion | flops 4297064448 | bytes 13631488 | tf_op jit(solution)/shard_map/dot_general | solution.py:13
  17.9 91.3 %reduce-scatter.2.cloned.1.call-done = bf16[512,512]{1,0:T(8,128)(2,1)} async-done(((bf16[512,4096]{1,0:T(8,128)(2,1)}), bf16[512,512]{1,0:T(8,128)(2,1)}) %reduce-scatter.2.cloned.1.call-update) | async-done | bytes 524304 | tf_op jit(solution)/shard_map/reduce_scatter | solution.py:50
  121.1 43.2 %all-gather.6.cloned.1.call-done = bf16[256,4096]{1,0:T(8,128)(2,1)} async-done(((bf16[256,512]{1,0:T(8,128)(2,1)}), bf16[256,4096]{1,0:T(8,128)(2,1)}) %all-gather.6.cloned.1.call-update) | async-done | bytes 2097168 | tf_op jit(solution)/shard_map/all_gather | solution.py:59
  173.8 11.4 %collective-permute-done.2 = bf16[2,512,512]{2,1,0:T(8,128)(2,1)S(1)} collective-permute-done((bf16[2,512,512]{2,1,0:T(8,128)(2,1)S(1)}, bf16[2,512,512]{2,1,0:T(8,128)(2,1)S(1)}, u32[]{:S(2)}, u32[]{:S(2)}) %collective-permute-start.2) | collective-permute-done | bytes 1048608 | tf_op jit(solution)/shard_map/ppermute | solution.py:56
  208.0 73.2 %collective-permute-done.4 = bf16[512,512]{1,0:T(8,128)(2,1)S(1)} collective-permute-done((bf16[512,512]{1,0:T(8,128)(2,1)S(1)}, bf16[512,512]{1,0:T(8,128)(2,1)S(1)}, u32[]{:S(2)}, u32[]{:S(2)}) %collective-permute-start.4) | collective-permute-done | bytes 524320 | tf_op jit(solution)/shard_map/ppermute | solution.py:22
  281.3 14.3 %all-gather.10.cloned.1.call-done = bf16[1024,8192]{1,0:T(8,128)(2,1)} async-done(((bf16[1024,512]{1,0:T(8,128)(2,1)}), bf16[1024,8192]{1,0:T(8,128)(2,1)}) %all-gather.10.cloned.1.call-update) | async-done | bytes 16777232 | tf_op jit(solution)/shard_map/all_gather | solution.py:82
  295.7 8.3 fusion.25
  318.9 107.5 %all-gather.12.cloned.1.call-done = bf16[1024,8192]{1,0:T(8,128)(2,1)} async-done(((bf16[1024,512]{1,0:T(8,128)(2,1)}), bf16[1024,8192]{1,0:T(8,128)(2,1)}) %all-gather.12.cloned.1.call-update) | async-done | bytes 16777232 | tf_op jit(solution)/shard_map/all_gather | solution.py:82
  426.4 8.3 fusion.13
  436.5 6.7 fusion.17
  449.7 107.4 %all-gather.14.cloned.1.call-done = bf16[1024,8192]{1,0:T(8,128)(2,1)} async-done(((bf16[1024,512]{1,0:T(8,128)(2,1)}), bf16[1024,8192]{1,0:T(8,128)(2,1)}) %all-gather.14.cloned.1.call-update) | async-done | bytes 16777232 | tf_op jit(solution)/shard_map/all_gather | solution.py:82
  557.0 8.4 %fusion.5 = f32[1024,512]{1,0:T(8,128)S(1)} fusion(bf16[4096,512]{1,0:T(8,128)(2,1)} %collective-permute-done.3, bf16[1024,8192]{1,0:T(8,128)(2,1)} %all-gather.14.cloned.1.call-done, s32[]{:T(128)S(6)} %select_n.73), kind=kOutput, calls=%fused_computation.10 | convolution fusion | flops 4294967296 | bytes 14680068 | tf_op jit(solution)/shard_map/dot_general | solution.py:13
  567.2 6.7 fusion.9
  589.5 98.3 %all-gather.8.cloned.1.call-done = bf16[1024,8192]{1,0:T(8,128)(2,1)} async-done(((bf16[1024,512]{1,0:T(8,128)(2,1)}), bf16[1024,8192]{1,0:T(8,128)(2,1)}) %all-gather.8.cloned.1.call-update) | async-done | bytes 16777232 | tf_op jit(solution)/shard_map/all_gather | solution.py:82
  687.7 8.3 fusion.29
  710.3 9.0 %fusion.31 = f32[1024,512]{1,0:T(8,128)S(1)} fusion(bf16[1024,8192]{1,0:T(8,128)(2,1)} %all-gather.8.cloned.1.call-done, s32[]{:T(128)S(6)} %select_n.72, bf16[1024,512]{1,0:T(8,128)(2,1)} %get-tuple-element.29, bf16[1024,512]{1,0:T(8,128)(2,1)} %get-tuple-element.31, bf16[1024,512]{1,0:T(8,128)(2,1)} %get-tuple-element.33, ...), kind=kOutput, calls=%fused_computation.36 | convolution fusion | flops 4311744512 | bytes 14680068 | tf_op jit(solution)/shard_map/dot_general | solution.py:13
  719.3 8.8 %fusion.23 = f32[1024,512]{1,0:T(8,128)S(1)} fusion(bf16[1024,8192]{1,0:T(8,128)(2,1)} %all-gather.10.cloned.1.call-done, s32[]{:T(128)S(6)} %select_n.72, bf16[1024,512]{1,0:T(8,128)(2,1)} %get-tuple-element.29, bf16[1024,512]{1,0:T(8,128)(2,1)} %get-tuple-element.31, bf16[1024,512]{1,0:T(8,128)(2,1)} %get-tuple-element.33, ...), kind=kOutput, calls=%fused_computation.28 | convolution fusion | flops 4311744512 | bytes 14680068 | tf_op jit(solution)/shard_map/dot_general | solution.py:13
  728.2 10.0 %fusion.15 = f32[1024,512]{1,0:T(8,128)} fusion(bf16[1024,8192]{1,0:T(8,128)(2,1)} %all-gather.12.cloned.1.call-done, s32[]{:T(128)S(6)} %select_n.72, bf16[1024,512]{1,0:T(8,128)(2,1)} %get-tuple-element.29, bf16[1024,512]{1,0:T(8,128)(2,1)} %get-tuple-element.31, bf16[1024,512]{1,0:T(8,128)(2,1)} %get-tuple-element.33, ...), kind=kOutput, calls=%fused_computation.20 | convolution fusion | flops 4311744512 | bytes 14680068 | tf_op jit(solution)/shard_map/dot_general | solution.py:13
  738.2 10.1 %fusion.7 = f32[1024,512]{1,0:T(8,128)} fusion(bf16[1024,8192]{1,0:T(8,128)(2,1)} %all-gather.14.cloned.1.call-done, s32[]{:T(128)S(6)} %select_n.72, bf16[1024,512]{1,0:T(8,128)(2,1)} %get-tuple-element.29, bf16[1024,512]{1,0:T(8,128)(2,1)} %get-tuple-element.31, bf16[1024,512]{1,0:T(8,128)(2,1)} %get-tuple-element.33, ...), kind=kOutput, calls=%fused_computation.12 | convolution fusion | flops 4311744512 | bytes 14680068 | tf_op jit(solution)/shard_map/dot_general | solution.py:13
  752.5 8.7 %fusion.27 = f32[1024,512]{1,0:T(8,128)S(1)} fusion(bf16[4096,512]{1,0:T(8,128)(2,1)S(1)} %constant_dynamic-update-slice_fusion, bf16[1024,8192]{1,0:T(8,128)(2,1)} %all-gather.8.cloned.1.call-done, s32[]{:T(128)S(6)} %select_n.73), kind=kOutput, calls=%fused_computation.32 | convolution fusion | flops 4294967296 | bytes 14680068 | tf_op jit(solution)/shard_map/dot_general | solution.py:13
  764.3 7.1 fusion.19
  775.8 8.3 fusion.11
  787.9 8.3 fusion.3
  820.8 14.1 %fusion = (f32[4096,512]{1,0:T(8,128)}, f32[4096,512]{1,0:T(8,128)}) fusion(f32[1024,512]{1,0:T(8,128)} %get-tuple-element.42, f32[1024,512]{1,0:T(8,128)} %get-tuple-element.41, f32[1024,512]{1,0:T(8,128)} %get-tuple-element.40, f32[1024,512]{1,0:T(8,128)} %get-tuple-element.39, f32[1024,512]{1,0:T(8,128)} %get-tuple-element.30, ...), kind=kLoop, calls=%fused_computation.2 | loop fusion | flops 20971520 | bytes 41943044 | tf_op jit(solution)/shard_map/sub | solution.py:123
  (142 shorter events, 133.9 us)
Async XLA Ops:
  7.2 101.9 %reduce-scatter.2.cloned.1.call-start = ((), (), s32[]{:S(2)}) async-start(), calls=%async_computation.1 | async-start | bytes 4718592 | tf_op jit(solution)/shard_map/reduce_scatter | solution.py:50
  17.8 146.4 %all-gather.6.cloned.1.call-start = ((), (), s32[]{:S(2)}) async-start(), calls=%async_computation.2 | async-start | bytes 2359296 | tf_op jit(solution)/shard_map/all_gather | solution.py:59
  110.5 2.0 collective-permute-start
  113.3 182.4 %all-gather.10.cloned.1.call-start = ((), (), s32[]{:S(2)}) async-start(), calls=%async_computation.4 | async-start | bytes 17825792 | tf_op jit(solution)/shard_map/all_gather | solution.py:82
  119.3 307.0 %all-gather.12.cloned.1.call-start = ((), (), s32[]{:S(2)}) async-start(), calls=%async_computation.5 | async-start | bytes 17825792 | tf_op jit(solution)/shard_map/all_gather | solution.py:82
  119.9 437.1 %all-gather.14.cloned.1.call-start = ((), (), s32[]{:S(2)}) async-start(), calls=%async_computation.6 | async-start | bytes 17825792 | tf_op jit(solution)/shard_map/all_gather | solution.py:82
  120.5 567.2 %all-gather.8.cloned.1.call-start = ((), (), s32[]{:S(2)}) async-start(), calls=%async_computation.3 | async-start | bytes 17825792 | tf_op jit(solution)/shard_map/all_gather | solution.py:82
  164.2 21.0 %collective-permute-start.1 = (bf16[256,4096]{1,0:T(8,128)(2,1)}, bf16[256,4096]{1,0:T(8,128)(2,1)}, u32[]{:S(2)}, u32[]{:S(2)}) collective-permute-start(bf16[256,4096]{1,0:T(8,128)(2,1)} %all-gather.6.cloned.1.call-done), channel_id=1, source_target_pairs={{0,16},{16,0},{1,17},{17,1},{2,18},{18,2},{3,19},{19,3},{4,20},{20... | collective-permute-start | bytes 6291464 | tf_op jit(solution)/shard_map/ppermute | solution.py:60
  164.3 20.8 %collective-permute-start.2 = (bf16[2,512,512]{2,1,0:T(8,128)(2,1)S(1)}, bf16[2,512,512]{2,1,0:T(8,128)(2,1)S(1)}, u32[]{:S(2)}, u32[]{:S(2)}) collective-permute-start(bf16[2,512,512]{2,1,0:T(8,128)(2,1)S(1)} %pad_maximum_fusion.6), channel_id=1, source_target_pairs={{0,1},{17,16},{2,3},{19,18},{4,5},{21,20},{6,7},{23,22},{8,9},{25,... | collective-permute-start | bytes 3145736 | tf_op jit(solution)/shard_map/ppermute | solution.py:56
  173.7 130.2 %collective-permute-start.3 = (bf16[4096,512]{1,0:T(8,128)(2,1)}, bf16[4096,512]{1,0:T(8,128)(2,1)}, u32[]{:S(2)}, u32[]{:S(2)}) collective-permute-start(bf16[4096,512]{1,0:T(8,128)(2,1)} %convert_element_type.57), channel_id=1, source_target_pairs={{0,1},{1,0},{2,3},{3,2},{4,5},{5,4},{6,7},{7,6},{8,9},{9,8},{10,11... | collective-permute-start | bytes 12582920 | tf_op jit(solution)/shard_map/ppermute | solution.py:22
  187.9 18.2 %copy-start.2 = (bf16[256,4096]{1,0:T(8,128)(2,1)}, bf16[256,4096]{1,0:T(8,128)(2,1)S(1)}, u32[]{:S(2)}) copy-start(bf16[256,4096]{1,0:T(8,128)(2,1)S(1)} %get-tuple-element.22) | copy-start | bytes 6291460
  193.4 87.8 %collective-permute-start.4 = (bf16[512,512]{1,0:T(8,128)(2,1)S(1)}, bf16[512,512]{1,0:T(8,128)(2,1)S(1)}, u32[]{:S(2)}, u32[]{:S(2)}) collective-permute-start(bf16[512,512]{1,0:T(8,128)(2,1)S(1)} %get-tuple-element.27), channel_id=1, source_target_pairs={{0,1},{1,0},{2,3},{3,2},{4,5},{5,4},{6,7},{7,6},{8,9},{9,8},{10,11... | collective-permute-start | bytes 1572872 | tf_op jit(solution)/shard_map/ppermute | solution.py:22
  317.5 431.1 %collective-permute-start.6 = (bf16[1024,512]{1,0:T(8,128)(2,1)}, bf16[1024,512]{1,0:T(8,128)(2,1)}, u32[]{:S(2)}, u32[]{:S(2)}) collective-permute-start(bf16[1024,512]{1,0:T(8,128)(2,1)} %get-tuple-element.33), channel_id=1, source_target_pairs={{0,1},{1,0},{2,3},{3,2},{4,5},{5,4},{6,7},{7,6},{8,9},{9,8},{10,11... | collective-permute-start | bytes 3145736 | tf_op jit(solution)/shard_map/ppermute | solution.py:22
  448.3 301.6 %collective-permute-start.7 = (bf16[1024,512]{1,0:T(8,128)(2,1)}, bf16[1024,512]{1,0:T(8,128)(2,1)}, u32[]{:S(2)}, u32[]{:S(2)}) collective-permute-start(bf16[1024,512]{1,0:T(8,128)(2,1)} %get-tuple-element.31), channel_id=1, source_target_pairs={{0,1},{1,0},{2,3},{3,2},{4,5},{5,4},{6,7},{7,6},{8,9},{9,8},{10,11... | collective-permute-start | bytes 3145736 | tf_op jit(solution)/shard_map/ppermute | solution.py:22
  579.2 171.9 %collective-permute-start.8 = (bf16[1024,512]{1,0:T(8,128)(2,1)}, bf16[1024,512]{1,0:T(8,128)(2,1)}, u32[]{:S(2)}, u32[]{:S(2)}) collective-permute-start(bf16[1024,512]{1,0:T(8,128)(2,1)} %get-tuple-element.29), channel_id=1, source_target_pairs={{0,1},{1,0},{2,3},{3,2},{4,5},{5,4},{6,7},{7,6},{8,9},{9,8},{10,11... | collective-permute-start | bytes 3145736 | tf_op jit(solution)/shard_map/ppermute | solution.py:22
  707.4 53.8 %copy-start.7 = (f32[1024,512]{1,0:T(8,128)}, f32[1024,512]{1,0:T(8,128)S(1)}, u32[]{:S(2)}) copy-start(f32[1024,512]{1,0:T(8,128)S(1)} %get-tuple-element.36) | copy-start | bytes 6291460
  707.4 41.1 %collective-permute-start.5 = (bf16[1024,512]{1,0:T(8,128)(2,1)S(1)}, bf16[1024,512]{1,0:T(8,128)(2,1)S(1)}, u32[]{:S(2)}, u32[]{:S(2)}) collective-permute-start(bf16[1024,512]{1,0:T(8,128)(2,1)S(1)} %get-tuple-element.35), channel_id=1, source_target_pairs={{0,1},{1,0},{2,3},{3,2},{4,5},{5,4},{6,7},{7,6},{8,9},{9,8},{10,11... | collective-permute-start | bytes 3145736 | tf_op jit(solution)/shard_map/ppermute | solution.py:22
  709.7 38.6 %collective-permute-start.9 = (bf16[512,512]{1,0:T(8,128)(2,1)S(1)}, bf16[512,512]{1,0:T(8,128)(2,1)S(1)}, u32[]{:S(2)}, u32[]{:S(2)}) collective-permute-start(bf16[512,512]{1,0:T(8,128)(2,1)S(1)} %get-tuple-element.37), channel_id=1, source_target_pairs={{0,1},{1,0},{2,3},{3,2},{4,5},{5,4},{6,7},{7,6},{8,9},{9,8},{10,11... | collective-permute-start | bytes 1572872 | tf_op jit(solution)/shard_map/ppermute | solution.py:22
  802.5 1.1 collective-permute-start.10
  803.7 3.5 collective-permute-start.11
  807.3 3.5 collective-permute-start.12
  810.9 3.5 collective-permute-start.13
  814.4 4.4 collective-permute-start.14
  820.8 14.1 %copy-start.1 = (bf16[1,512,1024]{2,1,0:T(8,128)(2,1)S(1)}, bf16[1,512,1024]{2,1,0:T(8,128)(2,1)}, u32[]{:S(2)}) copy-start(bf16[1,512,1024]{2,1,0:T(8,128)(2,1)} %param.6) | copy-start | bytes 3145732
  (27 other events, 211.9 us)
Sparse Core Ops, SparseCore 0:
  17.9 91.1 reduce-scatter.1
  113.4 50.8 all-gather.5
  167.1 128.5 all-gather.9
  297.8 128.5 all-gather.11
  428.5 128.5 all-gather.13
  559.2 128.5 all-gather.7

commit v2 on v1

--- a/solution.py
+++ b/solution.py
@@ -41,22 +41,57 @@
     return value.astype(bf16)
 
 
+def scatter_sum(part, axis):
+    n = lax.axis_size(axis)
+    me = lax.axis_index(axis)
+    share = part.shape[1] // n
+    blocks = [part[:, i * share:(i + 1) * share] for i in range(n)]
+    bit = 1
+    while bit < n:
+        mine = (me // bit) % 2 == 1
+        keep = [jnp.where(mine, high, low) for low, high in zip(blocks[0::2], blocks[1::2])]
+        send = [jnp.where(mine, low, high) for low, high in zip(blocks[0::2], blocks[1::2])]
+        send = jnp.concatenate([block.astype(bf16) for block in send], 1)
+        got = lax.ppermute(send, axis, [(i, i ^ bit) for i in range(n)]).astype(f32)
+        blocks = [block.astype(f32) + got[:, i * share:(i + 1) * share] for i, block in enumerate(keep)]
+        bit *= 2
+    return blocks[0]
+
+
+def gather_columns(block, axis):
+    n = lax.axis_size(axis)
+    me = lax.axis_index(axis)
+    bit = n // 2
+    blocks = [block]
+    while bit:
+        mine = (me // bit) % 2 == 1
+        own = jnp.concatenate(blocks, 1)
+        got = lax.ppermute(own, axis, [(i, i ^ bit) for i in range(n)])
+        share = block.shape[1]
+        got = [got[:, i * share:(i + 1) * share] for i in range(len(blocks))]
+        low = [jnp.where(mine, g, o) for g, o in zip(got, blocks)]
+        high = [jnp.where(mine, o, g) for g, o in zip(got, blocks)]
+        blocks = [x for pair in zip(low, high) for x in pair]
+        bit //= 2
+    return jnp.concatenate(blocks, 1)
+
+
 def make_states(context, out_weight, skip_states, width):
     n_tok, n_heads, n_mp = (lax.axis_size(a) for a in ("tok", "heads", "mp"))
     t, h, k = (lax.axis_index(a) for a in ("tok", "heads", "mp"))
     tokens, features = skip_states.shape[1:]
     share = features // n_heads
     part = dot(context[0], out_weight[0]).astype(bf16)
-    mine = lax.psum_scatter(part, "heads", scatter_dimension=1, tiled=True)
+    mine = scatter_sum(part, "heads")
     skip = lax.dynamic_slice(skip_states, (k, 0, h * share), (1, tokens, share))[0]
-    mine = (mine.astype(f32) + skip.astype(f32)).astype(bf16)
+    mine = (mine + skip.astype(f32)).astype(bf16)
     other = lax.ppermute(mine, "mp", [(0, 1), (1, 0)])
     pair = jnp.stack([jnp.where(k == 0, mine, other), jnp.where(k == 0, other, mine)])
     if share == width and n_tok == n_mp == 2:
         away = lax.ppermute(pair, ("mp", "tok"), [(0, 1), (3, 2)])
         columns = jnp.where(k == t, pair, away)
         half = lax.dynamic_slice_in_dim(pair[0], k * (tokens // 2), tokens // 2, 0)
-        rows = lax.all_gather(half, "heads", axis=1, tiled=True)
+        rows = gather_columns(half, "heads")
         rows_other = lax.ppermute(rows, "mp", [(0, 1), (1, 0)])
         first = jnp.where(k == 0, rows, rows_other)
         second = jnp.where(k == 0, rows_other, rows)
@@ -79,21 +114,22 @@
 
     map_half = map_old.astype(bf16)
     gram_old_half = gram_old.astype(bf16)
-    panels = [lax.all_gather(gram_old_half[cut], ("mp", "heads"), axis=1, tiled=True) for cut in cuts]
+    gram_old_half, context = lax.optimization_barrier((gram_old_half, context))
+    panel = lax.all_gather(gram_old_half, ("mp", "heads"), axis=1, tiled=True)
     maps = [map_half] + [shifted(map_half, "tok", s) for s in range(1, n_tok)]
     source, source_cols, target_cols = make_states(context, out_weight, skip_states, width)
 
     gram_new = decay_keep * gram_old + new_weight * token_inner(source, source_cols)
     cross_new = decay_keep * cross_old + new_weight * token_inner(source, target_cols)
 
-    def panel_part(panel, s):
+    def panel_part(cut, s):
         owner = lax.rem(t - s + n_tok, n_tok)
-        return lax.dynamic_slice_in_dim(panel, owner * height, height, 1)
+        return lax.dynamic_slice(panel, (cut.start, owner * height), (step, height))
 
     inner_map = sum_tok(dot(source, map_half))
     residuals, halves = [], []
-    for cut, panel in zip(cuts, panels):
-        product = sum(dot(panel_part(panel, s), maps[s]) for s in range(n_tok))
+    for cut in cuts:
+        product = sum(dot(panel_part(cut, s), maps[s]) for s in range(n_tok))
         low_rank = token_inner(source[:, cut], inner_map)
         residual = (
             cross_new[cut] - decay_keep * product - new_weight * low_rank - ridge_weight * map_old[cut]
@@ -104,8 +140,8 @@
     inner_residual = sum_tok(sum(dot(source[:, cut], half) for cut, half in zip(cuts, halves)))
     blocks = [jnp.concatenate(halves, 0)] + [jnp.concatenate(a, 0) for a in away]
     applied, squares, mixed = [], 0.0, 0.0
-    for cut, panel, residual in zip(cuts, panels, residuals):
-        product = sum(dot(panel_part(panel, s), blocks[s]) for s in range(n_tok))
+    for cut, residual in zip(cuts, residuals):
+        product = sum(dot(panel_part(cut, s), blocks[s]) for s in range(n_tok))
         low_rank = token_inner(source[:, cut], inner_residual)
         value = decay_keep * product + new_weight * low_rank + ridge_weight * residual
         applied.append(value)

time: 848 us -> 666 us (0.79)
  waiting for transfers between devices: 562 us -> 368 us
  other arithmetic: 30.7 us -> 40.3 us
  starting transfers between devices: 17.1 us -> 25.8 us
    all_gather x5 -> x1, waiting for transfers between devices: 371 us -> 0.02 us  [per_device(): panel = lax.all_gather(gram_old_half, ('mp', 'heads'), axis=1, tiled=True)]
    ppermute x0 -> x6, waiting for transfers between devices: none -> 267 us  [the longest x3 175 us: scatter_sum(): got = lax.ppermute(send, axis, [(i, i ^ bit) for i in range(n)]).astype(f32)]
    reduce_scatter x1 -> x0, waiting for transfers between devices: 91.3 us -> none  [make_states(): mine = lax.psum_scatter(part, 'heads', scatter_dimension=1, tiled=True)]
  transfers between devices with their start and end apart: 21 -> 22, of which waited for: 14 -> 14; matrix products, arithmetic and copies ran while one was open for 19% -> 25% of each run, Pallas kernels for 0% -> 0%
where the time goes in v2:
time: 666 us; the launch traced here: 658 us
  waiting for transfers between devices  368 us (55%)
  matrix products  195 us (29%)
  other arithmetic  40.3 us (6%)
  starting transfers between devices  25.8 us (4%)
  between operations  21.7 us (3%)
  local copies, waits for them, and re-layouts  7.34 us (1%)
    ppermute x3, waiting for transfers between devices, scatter_sum(): got = lax.ppermute(send, axis, [(i, i ^ bit) for i in range(n)]).astype(f32)  175 us
    dot_general x22, matrix products, dot(): return jnp.dot(a, b, preferred_element_type=f32)  161 us
    ppermute x3, waiting for transfers between devices, gather_columns(): got = lax.ppermute(own, axis, [(i, i ^ bit) for i in range(n)])  92.2 us
    ppermute x7, waiting for transfers between devices, shifted(): return lax.ppermute(block, axis, [(i, (i + shift) % n) for i in range(n)])  69 us
    dot_general x10, matrix products, token_inner(): lax.dot_general(left, right, (((0,), (0,)), ((), ())), preferred_element_...  33.4 us
    ppermute x1, waiting for transfers between devices, make_states(): away = lax.ppermute(pair, ('mp', 'tok'), [(0, 1), (3, 2)])  17.1 us
    sub x1, other arithmetic, per_device(): residual - step_size * jnp.concatenate(applied, 0)  14.1 us
  transfers between devices with their start and end apart: 22, of which 14 were waited for; matrix products, arithmetic and copies ran while one was open for 25% of the time, Pallas kernels for 0%

profile of v2, /device:TPU:0, one launch (start us, length us, event | category | flops | bytes accessed | tf_op | source)
XLA Modules:
  0.0 658.0 jit_solution(4569896277670211610)
XLA Ops:
  28.1 91.4 %collective-permute-done = bf16[512,2048]{1,0:T(8,128)(2,1)S(1)} collective-permute-done((bf16[512,2048]{1,0:T(8,128)(2,1)}, bf16[512,2048]{1,0:T(8,128)(2,1)S(1)}, u32[]{:S(2)}, u32[]{:S(2)}) %collective-permute-start) | collective-permute-done | bytes 2097184 | tf_op jit(solution)/shard_map/ppermute | solution.py:55
  122.3 48.0 %collective-permute-done.1 = bf16[512,1024]{1,0:T(8,128)(2,1)S(1)} collective-permute-done((bf16[512,1024]{1,0:T(8,128)(2,1)S(1)}, bf16[512,1024]{1,0:T(8,128)(2,1)S(1)}, u32[]{:S(2)}, u32[]{:S(2)}) %collective-permute-start.1) | collective-permute-done | bytes 1048608 | tf_op jit(solution)/shard_map/ppermute | solution.py:55
  177.6 35.3 %collective-permute-done.2 = bf16[512,512]{1,0:T(8,128)(2,1)S(1)} collective-permute-done((bf16[512,512]{1,0:T(8,128)(2,1)S(1)}, bf16[512,512]{1,0:T(8,128)(2,1)S(1)}, u32[]{:S(2)}, u32[]{:S(2)}) %collective-permute-start.2) | collective-permute-done | bytes 524320 | tf_op jit(solution)/shard_map/ppermute | solution.py:55
  216.4 20.9 %collective-permute-done.4 = bf16[256,512]{1,0:T(8,128)(2,1)S(1)} collective-permute-done((bf16[256,512]{1,0:T(8,128)(2,1)S(1)}, bf16[256,512]{1,0:T(8,128)(2,1)S(1)}, u32[]{:S(2)}, u32[]{:S(2)}) %collective-permute-start.4) | collective-permute-done | bytes 262176 | tf_op jit(solution)/shard_map/ppermute | solution.py:69
  237.6 25.5 %collective-permute-done.5 = bf16[256,1024]{1,0:T(8,128)(2,1)S(1)} collective-permute-done((bf16[256,1024]{1,0:T(8,128)(2,1)S(1)}, bf16[256,1024]{1,0:T(8,128)(2,1)S(1)}, u32[]{:S(2)}, u32[]{:S(2)}) %collective-permute-start.5) | collective-permute-done | bytes 524320 | tf_op jit(solution)/shard_map/ppermute | solution.py:69
  265.4 45.9 %collective-permute-done.6 = bf16[256,2048]{1,0:T(8,128)(2,1)S(1)} collective-permute-done((bf16[256,2048]{1,0:T(8,128)(2,1)S(1)}, bf16[256,2048]{1,0:T(8,128)(2,1)S(1)}, u32[]{:S(2)}, u32[]{:S(2)}) %collective-permute-start.6) | collective-permute-done | bytes 1048608 | tf_op jit(solution)/shard_map/ppermute | solution.py:69
  320.4 17.1 %collective-permute-done.8 = bf16[2,512,512]{2,1,0:T(8,128)(2,1)} collective-permute-done((bf16[2,512,512]{2,1,0:T(8,128)(2,1)}, bf16[2,512,512]{2,1,0:T(8,128)(2,1)}, u32[]{:S(2)}, u32[]{:S(2)}) %collective-permute-start.8) | collective-permute-done | bytes 1048608 | tf_op jit(solution)/shard_map/ppermute | solution.py:91
  361.4 69.0 %collective-permute-done.10 = bf16[512,512]{1,0:T(8,128)(2,1)S(1)} collective-permute-done((bf16[512,512]{1,0:T(8,128)(2,1)S(1)}, bf16[512,512]{1,0:T(8,128)(2,1)S(1)}, u32[]{:S(2)}, u32[]{:S(2)}) %collective-permute-start.10) | collective-permute-done | bytes 524320 | tf_op jit(solution)/shard_map/ppermute | solution.py:22
  430.7 8.3 %fusion.25 = f32[1024,512]{1,0:T(8,128)S(1)} fusion(bf16[4096,512]{1,0:T(8,128)(2,1)} %convert_element_type.93, bf16[4096,8192]{1,0:T(8,128)(2,1)} %all-gather.2.cloned.1.call-done, s32[]{:T(128)S(6)} %select_n.271), kind=kOutput, calls=%fused_computation.30 | convolution fusion | flops 4294967296 | bytes 14680068 | tf_op jit(solution)/shard_map/dot_general | solution.py:13
  439.0 8.3 %fusion.21 = f32[1024,512]{1,0:T(8,128)S(1)} fusion(bf16[4096,512]{1,0:T(8,128)(2,1)} %collective-permute-done.9, bf16[4096,8192]{1,0:T(8,128)(2,1)} %all-gather.2.cloned.1.call-done, s32[]{:T(128)S(6)} %select_n.272), kind=kOutput, calls=%fused_computation.26 | convolution fusion | flops 4294967296 | bytes 14680068 | tf_op jit(solution)/shard_map/dot_general | solution.py:13
  455.0 8.1 %fusion.13 = f32[1024,512]{1,0:T(8,128)S(1)} fusion(bf16[4096,512]{1,0:T(8,128)(2,1)} %collective-permute-done.9, bf16[4096,8192]{1,0:T(8,128)(2,1)} %all-gather.2.cloned.1.call-done, s32[]{:T(128)S(6)} %select_n.272), kind=kOutput, calls=%fused_computation.18 | convolution fusion | flops 4294967296 | bytes 14680068 | tf_op jit(solution)/shard_map/dot_general | solution.py:13
  463.2 8.2 %fusion.17 = f32[1024,512]{1,0:T(8,128)S(1)} fusion(bf16[4096,512]{1,0:T(8,128)(2,1)} %convert_element_type.93, bf16[4096,8192]{1,0:T(8,128)(2,1)} %all-gather.2.cloned.1.call-done, s32[]{:T(128)S(6)} %select_n.271), kind=kOutput, calls=%fused_computation.22 | convolution fusion | flops 4294967296 | bytes 14680068 | tf_op jit(solution)/shard_map/dot_general | solution.py:13
  478.0 8.3 %fusion.5 = f32[1024,512]{1,0:T(8,128)S(1)} fusion(bf16[4096,512]{1,0:T(8,128)(2,1)} %collective-permute-done.9, bf16[4096,8192]{1,0:T(8,128)(2,1)} %all-gather.2.cloned.1.call-done, s32[]{:T(128)S(6)} %select_n.272), kind=kOutput, calls=%fused_computation.10 | convolution fusion | flops 4294967296 | bytes 14680068 | tf_op jit(solution)/shard_map/dot_general | solution.py:13
  486.3 8.2 %fusion.9 = f32[1024,512]{1,0:T(8,128)S(1)} fusion(bf16[4096,512]{1,0:T(8,128)(2,1)} %convert_element_type.93, bf16[4096,8192]{1,0:T(8,128)(2,1)} %all-gather.2.cloned.1.call-done, s32[]{:T(128)S(6)} %select_n.271), kind=kOutput, calls=%fused_computation.14 | convolution fusion | flops 4294967296 | bytes 14680068 | tf_op jit(solution)/shard_map/dot_general | solution.py:13
  501.6 8.1 %fusion.29 = f32[1024,512]{1,0:T(8,128)S(1)} fusion(bf16[4096,512]{1,0:T(8,128)(2,1)} %collective-permute-done.9, bf16[4096,8192]{1,0:T(8,128)(2,1)} %all-gather.2.cloned.1.call-done, s32[]{:T(128)S(6)} %select_n.272), kind=kOutput, calls=%fused_computation.34 | convolution fusion | flops 4294967296 | bytes 14680068 | tf_op jit(solution)/shard_map/dot_general | solution.py:13
  509.8 10.6 %fusion.33 = f32[1024,512]{1,0:T(8,128)} fusion(bf16[4096,512]{1,0:T(8,128)(2,1)} %convert_element_type.93, bf16[4096,8192]{1,0:T(8,128)(2,1)} %all-gather.2.cloned.1.call-done, s32[]{:T(128)S(6)} %select_n.271), kind=kOutput, calls=%fused_computation.38 | convolution fusion | flops 4294967296 | bytes 14680068 | tf_op jit(solution)/shard_map/dot_general | solution.py:13
  526.3 8.8 %fusion.31 = f32[1024,512]{1,0:T(8,128)S(1)} fusion(bf16[4096,8192]{1,0:T(8,128)(2,1)} %all-gather.2.cloned.1.call-done, s32[]{:T(128)S(6)} %select_n.271, bf16[1024,512]{1,0:T(8,128)(2,1)} %get-tuple-element.46, bf16[1024,512]{1,0:T(8,128)(2,1)} %get-tuple-element.48, bf16[1024,512]{1,0:T(8,128)(2,1)} %get-tuple-element.50, ...), kind=kOutput, calls=%fused_computation.36 | convolution fusion | flops 4311744512 | bytes 14680068 | tf_op jit(solution)/shard_map/dot_general | solution.py:13
  535.1 9.1 %fusion.23 = f32[1024,512]{1,0:T(8,128)S(1)} fusion(bf16[4096,8192]{1,0:T(8,128)(2,1)} %all-gather.2.cloned.1.call-done, s32[]{:T(128)S(6)} %select_n.271, bf16[1024,512]{1,0:T(8,128)(2,1)} %get-tuple-element.46, bf16[1024,512]{1,0:T(8,128)(2,1)} %get-tuple-element.48, bf16[1024,512]{1,0:T(8,128)(2,1)} %get-tuple-element.50, ...), kind=kOutput, calls=%fused_computation.28 | convolution fusion | flops 4311744512 | bytes 14680068 | tf_op jit(solution)/shard_map/dot_general | solution.py:13
  544.2 10.0 %fusion.15 = f32[1024,512]{1,0:T(8,128)} fusion(bf16[4096,8192]{1,0:T(8,128)(2,1)} %all-gather.2.cloned.1.call-done, s32[]{:T(128)S(6)} %select_n.271, bf16[1024,512]{1,0:T(8,128)(2,1)} %get-tuple-element.46, bf16[1024,512]{1,0:T(8,128)(2,1)} %get-tuple-element.48, bf16[1024,512]{1,0:T(8,128)(2,1)} %get-tuple-element.50, ...), kind=kOutput, calls=%fused_computation.20 | convolution fusion | flops 4311744512 | bytes 14680068 | tf_op jit(solution)/shard_map/dot_general | solution.py:13
  554.2 10.0 %fusion.7 = f32[1024,512]{1,0:T(8,128)} fusion(bf16[4096,8192]{1,0:T(8,128)(2,1)} %all-gather.2.cloned.1.call-done, s32[]{:T(128)S(6)} %select_n.271, bf16[1024,512]{1,0:T(8,128)(2,1)} %get-tuple-element.46, bf16[1024,512]{1,0:T(8,128)(2,1)} %get-tuple-element.48, bf16[1024,512]{1,0:T(8,128)(2,1)} %get-tuple-element.50, ...), kind=kOutput, calls=%fused_computation.12 | convolution fusion | flops 4311744512 | bytes 14680068 | tf_op jit(solution)/shard_map/dot_general | solution.py:13
  568.4 8.4 %fusion.27 = f32[1024,512]{1,0:T(8,128)S(1)} fusion(bf16[4096,512]{1,0:T(8,128)(2,1)S(1)} %constant_dynamic-update-slice_fusion, bf16[4096,8192]{1,0:T(8,128)(2,1)} %all-gather.2.cloned.1.call-done, s32[]{:T(128)S(6)} %select_n.272), kind=kOutput, calls=%fused_computation.32 | convolution fusion | flops 4294967296 | bytes 14680068 | tf_op jit(solution)/shard_map/dot_general | solution.py:13
  591.7 8.3 %fusion.11 = f32[1024,512]{1,0:T(8,128)S(1)} fusion(bf16[4096,512]{1,0:T(8,128)(2,1)} %copy-done.24, bf16[4096,8192]{1,0:T(8,128)(2,1)} %all-gather.2.cloned.1.call-done, s32[]{:T(128)S(6)} %select_n.272), kind=kOutput, calls=%fused_computation.16 | convolution fusion | flops 4294967296 | bytes 14680068 | tf_op jit(solution)/shard_map/dot_general | solution.py:13
  603.8 8.3 %fusion.3 = f32[1024,512]{1,0:T(8,128)S(1)} fusion(bf16[4096,512]{1,0:T(8,128)(2,1)} %copy-done.24, bf16[4096,8192]{1,0:T(8,128)(2,1)} %all-gather.2.cloned.1.call-done, s32[]{:T(128)S(6)} %select_n.272), kind=kOutput, calls=%fused_computation.8 | convolution fusion | flops 4294967296 | bytes 14680068 | tf_op jit(solution)/shard_map/dot_general | solution.py:13
  636.7 14.1 %fusion = (f32[4096,512]{1,0:T(8,128)}, f32[4096,512]{1,0:T(8,128)}) fusion(f32[1024,512]{1,0:T(8,128)} %get-tuple-element.59, f32[1024,512]{1,0:T(8,128)} %get-tuple-element.58, f32[1024,512]{1,0:T(8,128)} %get-tuple-element.57, f32[1024,512]{1,0:T(8,128)} %get-tuple-element.56, f32[1024,512]{1,0:T(8,128)} %get-tuple-element.47, ...), kind=kLoop, calls=%fused_computation.2 | loop fusion | flops 20971520 | bytes 41943044 | tf_op jit(solution)/shard_map/sub | solution.py:159
  (170 shorter events, 138.1 us)
Async XLA Ops:
  7.2 423.5 %all-gather.2.cloned.1.call-start = ((), (), s32[]{:S(2)}) async-start(), calls=%async_computation | async-start | bytes 71303168 | tf_op jit(solution)/shard_map/all_gather | solution.py:118
  25.1 94.4 %collective-permute-start = (bf16[512,2048]{1,0:T(8,128)(2,1)}, bf16[512,2048]{1,0:T(8,128)(2,1)S(1)}, u32[]{:S(2)}, u32[]{:S(2)}) collective-permute-start(bf16[512,2048]{1,0:T(8,128)(2,1)} %pad_maximum_fusion.3), channel_id=1, source_target_pairs={{0,2},{2,0},{4,6},{6,4},{8,10},{10,8},{12,14},{14,12},{1,3},{3,1},... | collective-permute-start | bytes 6291464 | tf_op jit(solution)/shard_map/ppermute | solution.py:55
  122.2 48.1 %collective-permute-start.1 = (bf16[512,1024]{1,0:T(8,128)(2,1)S(1)}, bf16[512,1024]{1,0:T(8,128)(2,1)S(1)}, u32[]{:S(2)}, u32[]{:S(2)}) collective-permute-start(bf16[512,1024]{1,0:T(8,128)(2,1)S(1)} %pad_maximum_fusion.7), channel_id=1, source_target_pairs={{0,4},{2,6},{4,0},{6,2},{8,12},{10,14},{12,8},{14,10},{1,5},{3,7},... | collective-permute-start | bytes 3145736 | tf_op jit(solution)/shard_map/ppermute | solution.py:55
  175.7 37.2 %collective-permute-start.2 = (bf16[512,512]{1,0:T(8,128)(2,1)S(1)}, bf16[512,512]{1,0:T(8,128)(2,1)S(1)}, u32[]{:S(2)}, u32[]{:S(2)}) collective-permute-start(bf16[512,512]{1,0:T(8,128)(2,1)S(1)} %get-tuple-element.16), channel_id=1, source_target_pairs={{0,8},{2,10},{4,12},{6,14},{8,0},{10,2},{12,4},{14,6},{1,9},{3,11}... | collective-permute-start | bytes 1572872 | tf_op jit(solution)/shard_map/ppermute | solution.py:55
  214.3 2.0 collective-permute-start.3
  216.3 101.5 %slice-start = ((s8[8388608]{0:T(1024)(128)(4,1)}), s8[4194304]{0:T(1024)(128)(4,1)S(1)}, s32[]{:S(2)}) async-start(s8[8388608]{0:T(1024)(128)(4,1)} %bitcast.57), calls=%async_computation.1 | async-start | bytes 8388608
  216.4 20.9 %collective-permute-start.4 = (bf16[256,512]{1,0:T(8,128)(2,1)S(1)}, bf16[256,512]{1,0:T(8,128)(2,1)S(1)}, u32[]{:S(2)}, u32[]{:S(2)}) collective-permute-start(bf16[256,512]{1,0:T(8,128)(2,1)S(1)} %constant_dynamic-slice_fusion), channel_id=1, source_target_pairs={{0,8},{2,10},{4,12},{6,14},{8,0},{10,2},{12,4},{14,6},{1,9},{3,11}... | collective-permute-start | bytes 786440 | tf_op jit(solution)/shard_map/ppermute | solution.py:69
  237.5 25.6 %collective-permute-start.5 = (bf16[256,1024]{1,0:T(8,128)(2,1)S(1)}, bf16[256,1024]{1,0:T(8,128)(2,1)S(1)}, u32[]{:S(2)}, u32[]{:S(2)}) collective-permute-start(bf16[256,1024]{1,0:T(8,128)(2,1)S(1)} %pad_maximum_fusion.10), channel_id=1, source_target_pairs={{0,4},{2,6},{4,0},{6,2},{8,12},{10,14},{12,8},{14,10},{1,5},{3,7},... | collective-permute-start | bytes 1572872 | tf_op jit(solution)/shard_map/ppermute | solution.py:69
  263.3 48.0 %collective-permute-start.6 = (bf16[256,2048]{1,0:T(8,128)(2,1)S(1)}, bf16[256,2048]{1,0:T(8,128)(2,1)S(1)}, u32[]{:S(2)}, u32[]{:S(2)}) collective-permute-start(bf16[256,2048]{1,0:T(8,128)(2,1)S(1)} %pad_maximum_fusion.8), channel_id=1, source_target_pairs={{0,2},{2,0},{4,6},{6,4},{8,10},{10,8},{12,14},{14,12},{1,3},{3,1},... | collective-permute-start | bytes 3145736 | tf_op jit(solution)/shard_map/ppermute | solution.py:69
  312.0 25.6 %collective-permute-start.7 = (bf16[256,4096]{1,0:T(8,128)(2,1)S(1)}, bf16[256,4096]{1,0:T(8,128)(2,1)}, u32[]{:S(2)}, u32[]{:S(2)}) collective-permute-start(bf16[256,4096]{1,0:T(8,128)(2,1)S(1)} %select_dynamic-update-slice_fusion), channel_id=1, source_target_pairs={{0,16},{16,0},{1,17},{17,1},{2,18},{18,2},{3,19},{19,3},{4,20},{20... | collective-permute-start | bytes 6291464 | tf_op jit(solution)/shard_map/ppermute | solution.py:95
  313.3 24.1 %collective-permute-start.8 = (bf16[2,512,512]{2,1,0:T(8,128)(2,1)}, bf16[2,512,512]{2,1,0:T(8,128)(2,1)}, u32[]{:S(2)}, u32[]{:S(2)}) collective-permute-start(bf16[2,512,512]{2,1,0:T(8,128)(2,1)} %pad_maximum_fusion.9), channel_id=1, source_target_pairs={{0,1},{17,16},{2,3},{19,18},{4,5},{21,20},{6,7},{23,22},{8,9},{25,... | collective-permute-start | bytes 3145736 | tf_op jit(solution)/shard_map/ppermute | solution.py:91
  320.4 118.7 %collective-permute-start.9 = (bf16[4096,512]{1,0:T(8,128)(2,1)}, bf16[4096,512]{1,0:T(8,128)(2,1)}, u32[]{:S(2)}, u32[]{:S(2)}) collective-permute-start(bf16[4096,512]{1,0:T(8,128)(2,1)} %convert_element_type.93), channel_id=1, source_target_pairs={{0,1},{1,0},{2,3},{3,2},{4,5},{5,4},{6,7},{7,6},{8,9},{9,8},{10,11... | collective-permute-start | bytes 12582920 | tf_op jit(solution)/shard_map/ppermute | solution.py:22
  345.4 85.0 %collective-permute-start.10 = (bf16[512,512]{1,0:T(8,128)(2,1)S(1)}, bf16[512,512]{1,0:T(8,128)(2,1)S(1)}, u32[]{:S(2)}, u32[]{:S(2)}) collective-permute-start(bf16[512,512]{1,0:T(8,128)(2,1)S(1)} %get-tuple-element.44), channel_id=1, source_target_pairs={{0,1},{1,0},{2,3},{3,2},{4,5},{5,4},{6,7},{7,6},{8,9},{9,8},{10,11... | collective-permute-start | bytes 1572872 | tf_op jit(solution)/shard_map/ppermute | solution.py:22
  449.6 137.6 %copy-start.7 = (f32[1024,512]{1,0:T(8,128)}, f32[1024,512]{1,0:T(8,128)S(1)}, u32[]{:S(2)}) copy-start(f32[1024,512]{1,0:T(8,128)S(1)} %get-tuple-element.51) | copy-start | bytes 6291460
  449.6 114.9 %collective-permute-start.12 = (bf16[1024,512]{1,0:T(8,128)(2,1)}, bf16[1024,512]{1,0:T(8,128)(2,1)}, u32[]{:S(2)}, u32[]{:S(2)}) collective-permute-start(bf16[1024,512]{1,0:T(8,128)(2,1)} %get-tuple-element.50), channel_id=1, source_target_pairs={{0,1},{1,0},{2,3},{3,2},{4,5},{5,4},{6,7},{7,6},{8,9},{9,8},{10,11... | collective-permute-start | bytes 3145736 | tf_op jit(solution)/shard_map/ppermute | solution.py:22
  474.3 91.5 %collective-permute-start.13 = (bf16[1024,512]{1,0:T(8,128)(2,1)}, bf16[1024,512]{1,0:T(8,128)(2,1)}, u32[]{:S(2)}, u32[]{:S(2)}) collective-permute-start(bf16[1024,512]{1,0:T(8,128)(2,1)} %get-tuple-element.48), channel_id=1, source_target_pairs={{0,1},{1,0},{2,3},{3,2},{4,5},{5,4},{6,7},{7,6},{8,9},{9,8},{10,11... | collective-permute-start | bytes 3145736 | tf_op jit(solution)/shard_map/ppermute | solution.py:22
  497.3 69.8 %collective-permute-start.14 = (bf16[1024,512]{1,0:T(8,128)(2,1)}, bf16[1024,512]{1,0:T(8,128)(2,1)}, u32[]{:S(2)}, u32[]{:S(2)}) collective-permute-start(bf16[1024,512]{1,0:T(8,128)(2,1)} %get-tuple-element.46), channel_id=1, source_target_pairs={{0,1},{1,0},{2,3},{3,2},{4,5},{5,4},{6,7},{7,6},{8,9},{9,8},{10,11... | collective-permute-start | bytes 3145736 | tf_op jit(solution)/shard_map/ppermute | solution.py:22
  523.3 41.1 %collective-permute-start.11 = (bf16[1024,512]{1,0:T(8,128)(2,1)S(1)}, bf16[1024,512]{1,0:T(8,128)(2,1)S(1)}, u32[]{:S(2)}, u32[]{:S(2)}) collective-permute-start(bf16[1024,512]{1,0:T(8,128)(2,1)S(1)} %get-tuple-element.52), channel_id=1, source_target_pairs={{0,1},{1,0},{2,3},{3,2},{4,5},{5,4},{6,7},{7,6},{8,9},{9,8},{10,11... | collective-permute-start | bytes 3145736 | tf_op jit(solution)/shard_map/ppermute | solution.py:22
  524.9 39.3 %collective-permute-start.15 = (bf16[512,512]{1,0:T(8,128)(2,1)S(1)}, bf16[512,512]{1,0:T(8,128)(2,1)S(1)}, u32[]{:S(2)}, u32[]{:S(2)}) collective-permute-start(bf16[512,512]{1,0:T(8,128)(2,1)S(1)} %get-tuple-element.54), channel_id=1, source_target_pairs={{0,1},{1,0},{2,3},{3,2},{4,5},{5,4},{6,7},{7,6},{8,9},{9,8},{10,11... | collective-permute-start | bytes 1572872 | tf_op jit(solution)/shard_map/ppermute | solution.py:22
  618.4 1.1 collective-permute-start.16
  619.6 3.5 collective-permute-start.17
  623.2 3.5 collective-permute-start.18
  626.7 3.5 collective-permute-start.19
  630.3 4.4 collective-permute-start.20
  (33 other events, 494.6 us)
Sparse Core Ops, SparseCore 0:
  13.4 395.4 all-gather.1
